TPU v7x, 512 devices: a whole 4x4x16 slice. The times are simulated.
512 devices in a mesh: ctx: 32 (over x_lo, z), tp: 8 (over y, core), rep: 2 (over x_hi).
Axes of the slice: x: 4 (x_hi: 2, x_lo: 2; x = x_hi * 2 + x_lo), y: 4, z: 16, core: 2. Of those that a mesh axis runs over, the one named last changes fastest.
Arguments:
- queries: bfloat16 [1024, 16384], P(('rep', 'ctx'), 'tp'), parts along dimension 0, may hold values from -8 to 8
- cache_k: bfloat16 [32768, 1024], P(('rep', 'ctx'), 'tp'), parts along dimension 0, may hold values from -8 to 8
- cached_values: bfloat16 [32768, 1024], P(('rep', 'ctx'), 'tp'), parts along dimension 0, may hold values from -6 to 6
- new_token_keys: bfloat16 [1024, 1024], P(('rep', 'ctx'), 'tp'), parts along dimension 0, may hold values from -6 to 6
- new_token_values: bfloat16 [1024, 1024], P(('rep', 'ctx'), 'tp'), parts along dimension 0, may hold values from -6 to 6
- cache_lengths: int32 [64], P(('rep', 'ctx')), parts along dimension 0, may hold values from 2 to 512, as said below
- start_pos: int32 [2], P('rep'), parts along dimension 0, may hold values from 64 to 16384
- out_weight: bfloat16 [16384, 16384], P('tp', 'ctx'), may hold values from -0.046875 to 0.046875
Outputs:
- mixed: float32 [1024, 16384], P(('rep', 'tp'), 'ctx'), parts along dimension 0
There are 2 independent parts, one for each index of `rep`. A program takes and returns all parts, laid end to end along the dimension named above; an argument that names none is the same for every part. Nothing has to cross between parts.
Inputs may be any that keep to these rules, and one draw needn't show every extreme that they name: `cache_lengths`: some cache block is full, with 512 filled slots.
All inputs are finite; a program needn't handle non-finite values.
Results may differ from a plain program's by a relative error of at most 0.014.
Values may be sent and summed in bfloat16 or wider, within the bound.
No kernel may reach another device: no remote copies, remote signals or barrier semaphores. Data moves between devices by JAX's collectives and lax.ppermute only.
A program may use at most 64 MiB of HBM per device.

v0:
```python
import jax
import jax.numpy as jnp
from jax import lax
from jax.sharding import PartitionSpec as P

HEAD_SIZE = 128


far_away = 1073741824
very_low = -1e30


def head_split(row_matrix, kv_local):
    count_rows = row_matrix.shape[0]
    return row_matrix.reshape(
        count_rows, kv_local, row_matrix.shape[1] // (kv_local * HEAD_SIZE), HEAD_SIZE
    )


def empty_state(count_rows, kv_local, head_cluster):
    return (
        jnp.full((count_rows, kv_local, head_cluster), very_low, jnp.float32),
        jnp.zeros((count_rows, kv_local, head_cluster), jnp.float32),
        jnp.zeros((count_rows, kv_local, head_cluster, HEAD_SIZE), jnp.float32),
    )


def finish_block(state):
    run_max, run_sum, run_out = state
    block_norm = jnp.maximum(run_sum, 1.0)
    block_value = (run_out / block_norm[..., None]).astype(jnp.bfloat16)
    block_level = run_max + jnp.log(block_norm)
    return (block_value, block_level)


def fold_keys(running, query_mat, query_pos, key_mat, value_mat, key_pos, key_span):
    kv_local = key_mat.shape[1] // HEAD_SIZE
    tile_count = key_mat.shape[0] // key_span
    factor = HEAD_SIZE ** (-0.5)

    def update(carried, key_tile, value_tile, pos_tile):
        run_max, run_sum, run_out = carried
        scores = (
            jnp.einsum(
                "tkgd,skd->tkgs",
                query_mat,
                key_tile.reshape(key_span, kv_local, HEAD_SIZE),
                preferred_element_type=jnp.float32,
            )
            * factor
        )
        visible = pos_tile[None, None, None, :] <= query_pos[:, None, None, None]
        scores = jnp.where(visible, scores, very_low)
        new_max = jnp.maximum(run_max, jnp.max(scores, axis=-1))
        weights = jnp.where(visible, jnp.exp(scores - new_max[..., None]), 0.0)
        shrink = jnp.exp(run_max - new_max)
        new_sum = run_sum * shrink + jnp.sum(weights, axis=-1)
        new_out = run_out * shrink[..., None] + jnp.einsum(
            "tkgs,skd->tkgd",
            weights.astype(jnp.bfloat16),
            value_tile.reshape(key_span, kv_local, HEAD_SIZE),
            preferred_element_type=jnp.float32,
        )
        return (new_max, new_sum, new_out)

    def one_tile(tile_index, carried):
        key_tile = lax.dynamic_slice_in_dim(key_mat, tile_index * key_span, key_span, 0)
        value_tile = lax.dynamic_slice_in_dim(value_mat, tile_index * key_span, key_span, 0)
        pos_tile = lax.dynamic_slice_in_dim(key_pos, tile_index * key_span, key_span, 0)
        return update(carried, key_tile, value_tile, pos_tile)

    return lax.fori_loop(0, tile_count, one_tile, running)


def local(
    queries,
    cache_k,
    cached_values,
    new_token_keys,
    new_token_values,
    cache_lengths,
    start_pos,
    out_weight,
):
    cycle_size = lax.axis_size("ctx")
    my_place = lax.axis_index("ctx")
    query_rows = queries.shape[0]
    cache_rows = cache_k.shape[0]
    kv_local = cache_k.shape[1] // HEAD_SIZE
    head_cluster = queries.shape[1] // (kv_local * HEAD_SIZE)
    begin_pos = start_pos[0]
    slot_ids = jnp.arange(cache_rows, dtype=jnp.int32)
    slot_pos = slot_ids * cycle_size + my_place
    cache_pos = jnp.where(
        (slot_ids < cache_lengths[0]) & (slot_pos < begin_pos), slot_pos, far_away
    )
    stretch_pos = begin_pos + my_place * query_rows + jnp.arange(query_rows, dtype=jnp.int32)
    all_rows = query_rows * cycle_size
    key_span = min(128, cache_rows)
    query_piece = lax.all_gather(queries, "ctx", axis=0, tiled=True)
    piece_rows = query_piece.shape[0]
    piece_pos = begin_pos + jnp.arange(piece_rows, dtype=jnp.int32)
    query_mat = head_split(query_piece, kv_local)
    running = empty_state(piece_rows, kv_local, head_cluster)
    running = fold_keys(running, query_mat, piece_pos, cache_k, cached_values, cache_pos, key_span)
    running = fold_keys(
        running, query_mat, piece_pos, new_token_keys, new_token_values, stretch_pos, query_rows
    )
    block_state = tuple((new_part for new_part in running))
    block_value, block_level = finish_block(block_state)
    got_value = lax.all_to_all(
        block_value.reshape(all_rows, 1, -1), "ctx", split_axis=0, concat_axis=1, tiled=True
    )
    got_level = lax.all_to_all(block_level, "ctx", split_axis=0, concat_axis=1, tiled=True)
    got_value = got_value.reshape(query_rows, cycle_size, kv_local, head_cluster, HEAD_SIZE)
    got_level = got_level.reshape(query_rows, cycle_size, kv_local, head_cluster)
    top_level = jnp.max(got_level, axis=1, keepdims=True)
    scale_each = jnp.exp(got_level - top_level)
    total_scale = jnp.sum(scale_each, axis=1)
    joined = (
        jnp.sum(got_value.astype(jnp.float32) * scale_each[..., None], axis=1)
        / total_scale[..., None]
    )
    merged = joined.reshape(query_rows, -1).astype(jnp.bfloat16)
    term_rows = jnp.dot(
        lax.all_gather(merged, "ctx", axis=0, tiled=True),
        out_weight,
        preferred_element_type=jnp.float32,
    )
    return lax.psum_scatter(term_rows, "tp", scatter_dimension=0, tiled=True)


def solution(mesh):
    placed = (
        P(("rep", "ctx"), "tp"),
        P(("rep", "ctx"), "tp"),
        P(("rep", "ctx"), "tp"),
        P(("rep", "ctx"), "tp"),
        P(("rep", "ctx"), "tp"),
        P(("rep", "ctx")),
        P("rep"),
        P("tp", "ctx"),
    )
    return jax.shard_map(
        local, mesh=mesh, in_specs=placed, out_specs=P(("rep", "tp"), "ctx"), check_vma=False
    )
```

profile of v0, /device:TPU:6, one launch (start us, length us, event | category | flops | bytes accessed | tf_op | source)
XLA Modules:
  0.0 512.9 jit_solution(4798401228576427512)
XLA Ops:
  8.7 138.1 %all-gather.3.cloned.1.call-done = bf16[512,2048]{1,0:T(8,128)(2,1)} async-done(((bf16[16,2048]{1,0:T(8,128)(2,1)}), bf16[512,2048]{1,0:T(8,128)(2,1)}) %all-gather.3.cloned.1.call-update) | async-done | bytes 2097168 | tf_op jit(solution)/shard_map/all_gather | solution.py:100
  146.8 3.9 copy.36
  150.8 3.9 copy.37
  154.7 54.0 %while.5 = (s32[]{:T(128)}, f32[512,1,16]{0,2,1:T(8,128)S(1)}, f32[512,1,16]{0,2,1:T(8,128)S(1)}, f32[512,1,16,128]{0,3,2,1:T(8,128)}, s32[512]{0:T(512)S(1)}, /...) while((s32[]{:T(128)}, f32[512,1,16]{0,2,1:T(8,128)S(1)}, ...), condition=%wide.region_3.4_spmd.clone, body=%wide.region_0.3_spmd.clone.sunk | while | flops 553763328 | bytes 40703712 | solution.py:72
  155.5 4.4 fusion.63
  160.0 6.1 %bitcast_add_fusion.7 = f32[512,1,16,128]{0,3,2,1:T(8,128)} fusion(f32[512,1,16,128]{0,3,2,1:T(8,128)} %get-tuple-element.371, f32[128,512,16]{1,0,2:T(8,128)} %get-tuple-element.353, f32[512,16]{0,1:T(8,128)S(1)} %get-tuple-element.354, f32[512,16]{0,1:T(8,128)S(1)} %bitcast.162, pred[]{:T(512)S(6)} %compare.3, ...), kind=kOutput, calls=%fused_computation.1.clone.1 | convolution fusion | flops 276824064 | bytes 12746757 | tf_op jit(solution)/shard_map/while/body/eval_jaxpr/tkgs,skd->tkgd/dot_general | solution.py:58
  168.1 4.4 fusion.63
  172.5 7.4 %bitcast_add_fusion.7 = f32[512,1,16,128]{0,3,2,1:T(8,128)} fusion(f32[512,1,16,128]{0,3,2,1:T(8,128)} %get-tuple-element.371, f32[128,512,16]{1,0,2:T(8,128)} %get-tuple-element.353, f32[512,16]{0,1:T(8,128)S(1)} %get-tuple-element.354, f32[512,16]{0,1:T(8,128)S(1)} %bitcast.162, pred[]{:T(512)S(6)} %compare.3, ...), kind=kOutput, calls=%fused_computation.1.clone.1 | convolution fusion | flops 276824064 | bytes 12746757 | tf_op jit(solution)/shard_map/while/body/eval_jaxpr/tkgs,skd->tkgd/dot_general | solution.py:58
  181.9 4.4 fusion.63
  186.4 7.4 %bitcast_add_fusion.7 = f32[512,1,16,128]{0,3,2,1:T(8,128)} fusion(f32[512,1,16,128]{0,3,2,1:T(8,128)} %get-tuple-element.371, f32[128,512,16]{1,0,2:T(8,128)} %get-tuple-element.353, f32[512,16]{0,1:T(8,128)S(1)} %get-tuple-element.354, f32[512,16]{0,1:T(8,128)S(1)} %bitcast.162, pred[]{:T(512)S(6)} %compare.3, ...), kind=kOutput, calls=%fused_computation.1.clone.1 | convolution fusion | flops 276824064 | bytes 12746757 | tf_op jit(solution)/shard_map/while/body/eval_jaxpr/tkgs,skd->tkgd/dot_general | solution.py:58
  195.7 4.4 fusion.63
  200.2 7.4 %bitcast_add_fusion.7 = f32[512,1,16,128]{0,3,2,1:T(8,128)} fusion(f32[512,1,16,128]{0,3,2,1:T(8,128)} %get-tuple-element.371, f32[128,512,16]{1,0,2:T(8,128)} %get-tuple-element.353, f32[512,16]{0,1:T(8,128)S(1)} %get-tuple-element.354, f32[512,16]{0,1:T(8,128)S(1)} %bitcast.162, pred[]{:T(512)S(6)} %compare.3, ...), kind=kOutput, calls=%fused_computation.1.clone.1 | convolution fusion | flops 276824064 | bytes 12746757 | tf_op jit(solution)/shard_map/while/body/eval_jaxpr/tkgs,skd->tkgd/dot_general | solution.py:58
  213.0 6.4 %all-to-all-start.1 = ((f32[32,1,256]{2,1,0:T(1,128)}), f32[32,1,256]{2,1,0:T(1,128)S(1)}, u32[]{:S(2)}, u32[]{:S(2)}) async-start(f32[32,1,256]{2,1,0:T(1,128)} %reshape.198), calls=%async_computation.1 | async-start | bytes 65536 | tf_op jit(solution)/shard_map/all_to_all | solution.py:114
  219.4 4.5 fusion.27
  224.5 4.5 reduce.14
  229.0 4.0 copy.54
  232.9 4.5 reshape.200
  237.5 13.2 %all-to-all-start = ((bf16[32,2,16384]{2,1,0:T(2,128)(2,1)}), bf16[32,2,16384]{2,1,0:T(2,128)(2,1)}, u32[]{:S(2)}, u32[]{:S(2)}) async-start(bf16[32,2,16384]{2,1,0:T(2,128)(2,1)} %reshape.200), calls=%async_computation | async-start | bytes 4194304 | tf_op jit(solution)/shard_map/all_to_all | solution.py:111
  255.2 4.9 mul.119
  260.1 62.4 %all-to-all-done = bf16[32,2,16384]{2,1,0:T(2,128)(2,1)} async-done(((bf16[32,2,16384]{2,1,0:T(2,128)(2,1)}), bf16[32,2,16384]{2,1,0:T(2,128)(2,1)}, u32[]{:S(2)}, u32[]{:S(2)}) %all-to-all-start) | async-done | bytes 2097184 | tf_op jit(solution)/shard_map/all_to_all | solution.py:111
  322.5 10.5 %reshape.201 = bf16[512,1,2048]{2,1,0:T(2,128)(2,1)} reshape(bf16[32,2,16384]{2,1,0:T(2,128)(2,1)} %all-to-all-done) | data formatting | bytes 4194304
  338.1 130.8 %all-gather.5.cloned.1.call-done = bf16[512,2048]{1,0:T(8,128)(2,1)} async-done(((bf16[16,2048]{1,0:T(8,128)(2,1)}), bf16[512,2048]{1,0:T(8,128)(2,1)}) %all-gather.5.cloned.1.call-update) | async-done | bytes 2097168 | tf_op jit(solution)/shard_map/all_gather | solution.py:126
  468.9 3.8 fusion.52
  472.7 33.7 %reduce-scatter.2.cloned.1.call-done = f32[64,512]{1,0:T(8,128)} async-done(((f32[512,512]{1,0:T(8,128)}), f32[64,512]{1,0:T(8,128)}) %reduce-scatter.2.cloned.1.call-update) | async-done | bytes 131088 | tf_op jit(solution)/shard_map/reduce_scatter | solution.py:130
  (79 shorter events, 22.9 us)
Async XLA Ops:
  6.5 462.4 %copy-start = (bf16[2048,512]{1,0:T(8,128)(2,1)S(1)}, bf16[2048,512]{1,0:T(8,128)(2,1)}, u32[]{:S(2)}) copy-start(bf16[2048,512]{1,0:T(8,128)(2,1)} %param.17) | copy-start | bytes 6291460
  6.5 140.3 %all-gather.3.cloned.1.call-start = ((), (), s32[]{:S(2)}) async-start(), calls=%async_computation.3 | async-start | bytes 2162688 | tf_op jit(solution)/shard_map/all_gather | solution.py:100
  154.7 54.1 %copy-start.3 = (bf16[16,128]{1,0:T(8,128)(2,1)S(1)}, bf16[16,128]{1,0:T(8,128)(2,1)}, u32[]{:S(2)}) copy-start(bf16[16,128]{1,0:T(8,128)(2,1)} %param.13) | copy-start | bytes 12292
  160.0 6.1 %copy-start.1 = (f32[128,512,16]{1,0,2:T(8,128)S(1)}, f32[128,512,16]{1,0,2:T(8,128)}, u32[]{:S(2)}) copy-start(f32[128,512,16]{1,0,2:T(8,128)} %get-tuple-element.353) | copy-start | bytes 12582916 | tf_op jit(solution)/shard_map/while
  172.5 7.4 %copy-start.1 = (f32[128,512,16]{1,0,2:T(8,128)S(1)}, f32[128,512,16]{1,0,2:T(8,128)}, u32[]{:S(2)}) copy-start(f32[128,512,16]{1,0,2:T(8,128)} %get-tuple-element.353) | copy-start | bytes 12582916 | tf_op jit(solution)/shard_map/while
  186.4 7.4 %copy-start.1 = (f32[128,512,16]{1,0,2:T(8,128)S(1)}, f32[128,512,16]{1,0,2:T(8,128)}, u32[]{:S(2)}) copy-start(f32[128,512,16]{1,0,2:T(8,128)} %get-tuple-element.353) | copy-start | bytes 12582916 | tf_op jit(solution)/shard_map/while
  200.2 7.4 %copy-start.1 = (f32[128,512,16]{1,0,2:T(8,128)S(1)}, f32[128,512,16]{1,0,2:T(8,128)}, u32[]{:S(2)}) copy-start(f32[128,512,16]{1,0,2:T(8,128)} %get-tuple-element.353) | copy-start | bytes 12582916 | tf_op jit(solution)/shard_map/while
  208.7 10.7 %copy-start.4 = (bf16[16,128]{1,0:T(8,128)(2,1)S(1)}, bf16[16,128]{1,0:T(8,128)(2,1)}, u32[]{:S(2)}) copy-start(bf16[16,128]{1,0:T(8,128)(2,1)} %param.14) | copy-start | bytes 12292
  213.0 24.5 %all-to-all-start.1 = ((f32[32,1,256]{2,1,0:T(1,128)}), f32[32,1,256]{2,1,0:T(1,128)S(1)}, u32[]{:S(2)}, u32[]{:S(2)}) async-start(f32[32,1,256]{2,1,0:T(1,128)} %reshape.198), calls=%async_computation.1 | async-start | bytes 65536 | tf_op jit(solution)/shard_map/all_to_all | solution.py:114
  237.5 85.0 %all-to-all-start = ((bf16[32,2,16384]{2,1,0:T(2,128)(2,1)}), bf16[32,2,16384]{2,1,0:T(2,128)(2,1)}, u32[]{:S(2)}, u32[]{:S(2)}) async-start(bf16[32,2,16384]{2,1,0:T(2,128)(2,1)} %reshape.200), calls=%async_computation | async-start | bytes 4194304 | tf_op jit(solution)/shard_map/all_to_all | solution.py:111
  250.7 218.2 %all-gather.5.cloned.1.call-start = ((), (), s32[]{:S(2)}) async-start(), calls=%async_computation.4 | async-start | bytes 2162688 | tf_op jit(solution)/shard_map/all_gather | solution.py:126
  333.0 3.6 copy-start.2
  338.0 168.4 %reduce-scatter.2.cloned.1.call-start = ((), (), s32[]{:S(2)}) async-start(), calls=%async_computation.5 | async-start | bytes 1179648 | tf_op jit(solution)/shard_map/reduce_scatter | solution.py:130
Sparse Core Ops, SparseCore 0:
  9.4 137.3 all-gather.2
  338.1 130.7 all-gather.4
  472.9 33.5 reduce-scatter.1
where the time goes:
time: 514 us; the launch traced here: 513 us
  waiting for transfers between devices  366 us (71%)
  matrix products  56.4 us (11%)
  local copies, waits for them, and re-layouts  41.2 us (8%)
  starting transfers between devices  19.9 us (4%)
  other arithmetic  14.8 us (3%)
  between operations  14.6 us (3%)
    all_gather x1, waiting for transfers between devices, local(): query_piece = lax.all_gather(queries, 'ctx', axis=0, tiled=True)  138 us
    all_gather x1, waiting for transfers between devices, local(): lax.all_gather(merged, 'ctx', axis=0, tiled=True)  131 us
    all_to_all x1, waiting for transfers between devices, local(): lax.all_to_all(block_value.reshape(all_rows, 1, -1), 'ctx', split_axis=0,...  62.4 us
    reduce_scatter x1, waiting for transfers between devices, local(): return lax.psum_scatter(term_rows, 'tp', scatter_dimension=0, tiled=True)  33.7 us
    dot_general x5, matrix products, update(): jnp.einsum('tkgs,skd->tkgd', weights.astype(jnp.bfloat16), value_tile.res...  32.8 us
    unnamed x15, local copies, waits for them, and re-layouts  24.3 us
    dot_general x5, matrix products, update(): jnp.einsum('tkgd,skd->tkgs', query_mat, key_tile.reshape(key_span, kv_loc...  19.7 us
    all_to_all x1, starting transfers between devices, local(): lax.all_to_all(block_value.reshape(all_rows, 1, -1), 'ctx', split_axis=0,...  13.2 us
  transfers between devices with their start and end apart: 5, of which 4 were waited for; matrix products, arithmetic and copies ran while one was open for 5% of the time, Pallas kernels for 0%

commit v1 on v0

v1 whole, which is shorter than its diff:
```python
import functools

import jax
import jax.numpy as jnp
import numpy as np
from jax import lax
from jax.experimental import pallas as pl
from jax.experimental.pallas import tpu as pltpu
from jax.sharding import PartitionSpec as P

HEAD_SIZE = 128
RING = 16
LANES = 128
very_low = -1e30
far_away = 1073741824
FACTOR = float(HEAD_SIZE ** (-0.5) * np.log2(np.e))
VMEM_LIMIT = 48 * 1024 * 1024


SHARERS = (0, 1, RING, RING + 1)
ACROSS = [(c, c ^ RING) for c in range(2 * RING)]
EIGHTS = [[x * RING + p + 2 * i for i in range(RING // 2)] for x in range(2) for p in range(2)]
RINGS = [[x * RING + z for z in range(RING)] for x in range(2)]
WIRE = jnp.float16
QUERY_SCALE = 4096.0
ROW_TOP = 13


def vmem_specs(count):
    return [pl.BlockSpec(memory_space=pltpu.VMEM)] * count


PARAMS = pltpu.CompilerParams(vmem_limit_bytes=VMEM_LIMIT)


def pack_kernel(length_ref, k_ref, nk_ref, v_ref, nv_ref, o_ref, sems):
    cached, rows = k_ref.shape[0], nk_ref.shape[0]
    copies, start = [], 0
    for i, ref in enumerate((k_ref, nk_ref, v_ref, nv_ref)):
        size = ref.shape[0]
        copies.append(
            pltpu.make_async_copy(ref, o_ref.at[pl.ds(start, size)], sems.at[i])
        )
        copies[-1].start()
        start += size
    row = lax.broadcasted_iota(jnp.int32, (16, LANES), 0)
    filled = length_ref[0]
    digit = jnp.where(row < 8, filled // 16, filled % 16)
    o_ref[2 * (cached + rows) :] = digit.astype(jnp.float32).astype(jnp.bfloat16)
    for copy in copies:
        copy.wait()


def pack(length, k, nk, v, nv):
    total = 2 * (k.shape[0] + nk.shape[0]) + 16
    return pl.pallas_call(
        pack_kernel,
        out_shape=jax.ShapeDtypeStruct((total, LANES), jnp.bfloat16),
        in_specs=[pl.BlockSpec(memory_space=pltpu.SMEM)]
        + [pl.BlockSpec(memory_space=pltpu.HBM)] * 4,
        out_specs=pl.BlockSpec(memory_space=pltpu.VMEM),
        scratch_shapes=[pltpu.SemaphoreType.DMA((4,))],
        compiler_params=PARAMS,
        name="pack",
    )(length, k, nk, v, nv)


def attend_kernel(heads, rows, cached, sizes, place_ref, q_ref, *refs):
    kv_refs = refs[: len(SHARERS)]
    o_ref, k_all, v_all = refs[len(SHARERS) :]
    begin, me = place_ref[0], place_ref[1]
    span = cached + rows
    fresh = len(SHARERS) * rows
    cycle = 2 * RING
    keys = k_all.shape[0]

    k_all[cached:] = jnp.zeros((keys - cached, HEAD_SIZE), jnp.bfloat16)
    v_all[cached:, :HEAD_SIZE] = jnp.zeros((keys - cached, HEAD_SIZE), jnp.bfloat16)
    v_all[:, HEAD_SIZE:] = jnp.ones((keys, HEAD_SIZE), jnp.bfloat16)
    lane = lax.broadcasted_iota(jnp.int32, (1, LANES), 1)
    new_pos = jnp.full((1, LANES), far_away, jnp.int32)
    starts, ends = [], []
    end = fresh
    for i, (sharer, ref) in enumerate(zip(SHARERS, kv_refs)):
        index = jnp.bitwise_xor(me, sharer)
        at = slice(i * rows, (i + 1) * rows)
        k_all[at] = ref[cached:span]
        v_all[at, :HEAD_SIZE] = ref[span + cached : 2 * span]
        new_pos = jnp.where(
            (lane >= i * rows) & (lane < (i + 1) * rows), index * rows + lane - i * rows, new_pos
        )
        digits = ref[2 * span :].astype(jnp.float32)
        filled = jnp.max(digits[:1] * 16 + digits[8:9]).astype(jnp.int32)
        live = jnp.minimum(filled, (begin - index + cycle - 1) // cycle)
        to = pl.ds(pl.multiple_of(end, 16), cached)
        k_all[to, :] = ref[:cached]
        v_all[to, :HEAD_SIZE] = ref[span : span + cached]
        starts.append(end)
        ends.append(end + live)
        end = end + (live + 15) // 16 * 16

    token = lax.broadcasted_iota(jnp.int32, (heads * rows, LANES), 0) % rows
    lanes = lax.broadcasted_iota(jnp.int32, (rows, LANES), 1)
    parity, x = me % 2, me // RING

    def run(size):
        slot = lax.broadcasted_iota(jnp.int32, (1, size), 1)
        seen = functools.reduce(
            jnp.logical_or, [(slot >= a) & (slot < b) for a, b in zip(starts, ends)]
        )
        bias = jnp.where(seen, 0.0, very_low)

        def one(chunk):
            at = pl.ds(pl.multiple_of(chunk * rows, rows), rows)
            query = jnp.concatenate(
                [q_ref[at, h * HEAD_SIZE : (h + 1) * HEAD_SIZE] for h in range(heads)], axis=0
            )
            scores = lax.dot_general(
                query, k_all[:size], (((1,), (1,)), ((), ())), preferred_element_type=jnp.float32
            )
            old = scores[:, LANES:] + bias[:, LANES:]
            first = scores[:, :LANES]
            owner = x * RING + parity + 2 * chunk
            visible = new_pos <= token + owner * rows
            mixed = jnp.where(lane < fresh, jnp.where(visible, first, very_low), first + bias[:, :LANES])
            top = jnp.maximum(
                jnp.max(old, axis=1, keepdims=True), jnp.max(mixed, axis=1, keepdims=True)
            )
            weights = jnp.concatenate(
                [
                    jnp.exp2((mixed - top) * FACTOR).astype(jnp.bfloat16),
                    jnp.exp2((old - top) * FACTOR).astype(jnp.bfloat16),
                ],
                axis=1,
            )
            both = jnp.dot(weights, v_all[:size], preferred_element_type=jnp.float32)
            norm = both[:, HEAD_SIZE:]
            value = both[:, :HEAD_SIZE] / norm
            level = top * FACTOR + jnp.log2(norm)
            packed = jnp.zeros((rows, LANES), jnp.float32)
            for h in range(heads):
                part = slice(h * rows, (h + 1) * rows)
                o_ref[at, h * HEAD_SIZE : (h + 1) * HEAD_SIZE] = value[part].astype(jnp.bfloat16)
                packed = jnp.where(lanes == h, level[part], packed)
            o_ref[at, heads * HEAD_SIZE :] = pack_level(packed)

        @pl.loop(0, RING // 4)
        def _(pair):
            one(2 * pair)
            one(2 * pair + 1)

    below = 0
    for size in sizes:
        pl.when((end > below) & (end <= size))(functools.partial(run, size))
        below = size


def attend(position, gathered, blocks, rows):
    count, width = gathered.shape
    heads = width // HEAD_SIZE
    cached = (blocks[0].shape[0] - 16) // 2 - rows
    most = -(-len(blocks) * (cached + rows) // LANES) * LANES
    sizes = tuple(-(-most * i // 4 // LANES) * LANES for i in (1, 2, 3, 4))
    return pl.pallas_call(
        functools.partial(attend_kernel, heads, rows, cached, sizes),
        out_shape=jax.ShapeDtypeStruct((count, width + LANES), jnp.bfloat16),
        in_specs=[pl.BlockSpec(memory_space=pltpu.SMEM)] + vmem_specs(1 + len(blocks)),
        out_specs=pl.BlockSpec(memory_space=pltpu.VMEM),
        scratch_shapes=[
            pltpu.VMEM((most, HEAD_SIZE), jnp.bfloat16),
            pltpu.VMEM((most, 2 * HEAD_SIZE), jnp.bfloat16),
        ],
        compiler_params=PARAMS,
        cost_estimate=pl.CostEstimate(
            flops=6 * count * heads * most * HEAD_SIZE,
            bytes_accessed=4 << 20,
            transcendentals=count * heads * most,
        ),
        name="attend",
    )(position, gathered, *blocks)


def pack_level(level):
    high = level.astype(jnp.bfloat16).astype(jnp.float32)
    middle = (level - high).astype(jnp.bfloat16).astype(jnp.float32)
    low = (level - high - middle).astype(jnp.bfloat16).astype(jnp.float32)
    spread = high + pltpu.roll(middle, 32, 1) + pltpu.roll(low, 64, 1)
    return spread.astype(jnp.bfloat16)


def unpack_level(spread):
    spread = spread.astype(jnp.float32)
    return spread + pltpu.roll(spread, 96, 1) + pltpu.roll(spread, 64, 1)


def merge_kernel(rows, heads, parts_ref, o_ref, value_ref):
    lane = lax.broadcasted_iota(jnp.int32, (rows, LANES), 1)
    parts = [slice(i * rows, (i + 1) * rows) for i in range(parts_ref.shape[0] // rows)]
    levels = [unpack_level(parts_ref[at, heads * HEAD_SIZE :]) for at in parts]
    top = functools.reduce(jnp.maximum, levels)
    weights = [jnp.exp2(level - top) for level in levels]
    total = 1 / sum(weights)
    scales = [weight * total for weight in weights]
    largest = jnp.zeros((rows, HEAD_SIZE), jnp.float32)
    for h in range(heads):
        span = slice(h * HEAD_SIZE, (h + 1) * HEAD_SIZE)
        value = sum(
            parts_ref[at, span].astype(jnp.float32) * scale[:, h : h + 1]
            for at, scale in zip(parts, scales)
        )
        value_ref[:, span] = value
        largest = jnp.maximum(largest, jnp.abs(value))
    largest = jnp.max(largest, axis=1, keepdims=True)
    power = jnp.floor(jnp.log2(jnp.maximum(largest, 1e-30)))
    o_ref[:, : heads * HEAD_SIZE] = value_ref[...] * jnp.exp2(ROW_TOP - power)
    o_ref[:, heads * HEAD_SIZE :] = jnp.where(lane >= 0, power, 0.0)


def merge(parts, rows):
    width = parts.shape[1]
    heads = width // HEAD_SIZE - 1
    return pl.pallas_call(
        functools.partial(merge_kernel, rows, heads),
        out_shape=jax.ShapeDtypeStruct((rows, width), jnp.float32),
        in_specs=vmem_specs(1),
        out_specs=pl.BlockSpec(memory_space=pltpu.VMEM),
        scratch_shapes=[pltpu.VMEM((rows, heads * HEAD_SIZE), jnp.float32)],
        compiler_params=PARAMS,
        name="merge",
    )(parts)


def attention(
    queries,
    cache_k,
    cached_values,
    new_token_keys,
    new_token_values,
    cache_lengths,
    start_pos,
):
    me = lax.axis_index("ctx")
    rows = queries.shape[0]
    mine = pack(cache_lengths, cache_k, new_token_keys, cached_values, new_token_values)
    blocks = [mine] + [
        lax.ppermute(mine, "ctx", [(c, c ^ sharer) for c in range(2 * RING)])
        for sharer in SHARERS[1:]
    ]
    gathered = lax.all_gather(
        (queries.astype(jnp.float32) * QUERY_SCALE).astype(WIRE),
        "ctx", axis=0, tiled=True, axis_index_groups=EIGHTS,
    )
    gathered = (gathered.astype(jnp.float32) * (1 / QUERY_SCALE)).astype(jnp.bfloat16)
    position = jnp.stack([start_pos[0], me]).astype(jnp.int32)
    parts = attend(position, gathered, blocks, rows)
    parts = lax.all_to_all(parts, "ctx", 0, 0, tiled=True, axis_index_groups=EIGHTS)
    return merge(parts, rows), gathered


def attended_rows(scaled):
    rows = scaled[:, :-LANES].astype(jnp.float32) * jnp.exp2(
        scaled[:, -LANES : 1 - LANES].astype(jnp.float32) - ROW_TOP
    )
    return rows.astype(jnp.bfloat16)


def project_kernel(place_ref, rows_ref, weight_ref, their_ref, o_ref):
    x = place_ref[0]
    height = rows_ref.shape[0]
    for ref, column in ((weight_ref, x), (their_ref, 1 - x)):
        at = pl.ds(pl.multiple_of(column * height, height), height)
        o_ref[at, :] = jnp.dot(
            rows_ref[...], ref[...], preferred_element_type=jnp.float32
        ).astype(jnp.bfloat16)


def project(x, rows, weight, theirs):
    height, depth = rows.shape
    width = weight.shape[1]
    return pl.pallas_call(
        project_kernel,
        out_shape=jax.ShapeDtypeStruct((2 * height, width), jnp.bfloat16),
        in_specs=[pl.BlockSpec(memory_space=pltpu.SMEM)] + vmem_specs(3),
        out_specs=pl.BlockSpec(memory_space=pltpu.VMEM),
        compiler_params=PARAMS,
        cost_estimate=pl.CostEstimate(
            flops=4 * height * depth * width, bytes_accessed=6 << 20, transcendentals=0
        ),
        name="project",
    )(x, rows, weight, theirs)


def local(*arguments):
    out_weight = arguments[-1]
    scaled, first = attention(*arguments[:-1])
    their_weight, _ = lax.optimization_barrier((out_weight, first))
    their_weight = lax.ppermute(their_weight, "ctx", ACROSS)
    scaled = lax.all_gather(
        scaled.astype(WIRE), "ctx", axis=0, tiled=True, axis_index_groups=RINGS
    )
    x = (lax.axis_index("ctx") // RING).astype(jnp.int32).reshape(1)
    terms = project(x, attended_rows(scaled), out_weight, their_weight)
    terms = lax.all_to_all(terms.reshape(8, -1, terms.shape[1]), "tp", 0, 0, tiled=True)
    block = jnp.sum(terms.astype(jnp.float32), axis=0)
    home = [
        ((x * RING + z) * 8 + j, ((j // 4) * RING + z) * 8 + 4 * x + j % 4)
        for x in range(2)
        for z in range(RING)
        for j in range(8)
    ]
    return lax.ppermute(block, ("ctx", "tp"), home)


def solution(mesh):
    placed = (
        P(("rep", "ctx"), "tp"),
        P(("rep", "ctx"), "tp"),
        P(("rep", "ctx"), "tp"),
        P(("rep", "ctx"), "tp"),
        P(("rep", "ctx"), "tp"),
        P(("rep", "ctx")),
        P("rep"),
        P("tp", "ctx"),
    )
    return jax.shard_map(
        local, mesh=mesh, in_specs=placed, out_specs=P(("rep", "tp"), "ctx"), check_vma=False
    )
```

time: 514 us -> 158 us (0.31)
  waiting for transfers between devices: 366 us -> 29.4 us
  blocking collectives: 0 us -> 87.2 us
  matrix products: 56.4 us -> 0 us
  local copies, waits for them, and re-layouts: 41.2 us -> 3.83 us
  other arithmetic: 14.8 us -> 1.49 us
  between operations: 14.6 us -> 1.45 us
  Pallas kernels: 0 us -> 11 us
    all_gather x2 -> x0, waiting for transfers between devices: 269 us -> none  [the longest x1 138 us: local(): query_piece = lax.all_gather(queries, 'ctx', axis=0, tiled=True)]
    all_gather x0 -> x2, blocking collectives: none -> 73.1 us  [the longest x1 39.9 us: attention(): lax.all_gather((queries.astype(jnp.float32) * QUERY_SCALE).astype(WIRE),...]
    dot_general x11 -> x0, matrix products: 56.4 us -> none  [the longest x5 32.8 us: update(): jnp.einsum('tkgs,skd->tkgd', weights.astype(jnp.bfloat16), value_tile.res...]
    all_to_all x2 -> x1, waiting for transfers between devices: 62.4 us -> 24.1 us  [attention(): lax.all_to_all(parts, 'ctx', 0, 0, tiled=True, axis_index_groups=EIGHTS)]
    reduce_scatter x1 -> x0, waiting for transfers between devices: 33.7 us -> none  [local(): return lax.psum_scatter(term_rows, 'tp', scatter_dimension=0, tiled=True)]
    unnamed x15 -> x11, local copies, waits for them, and re-layouts: 24.3 us -> 3.83 us
    ppermute x0 -> x5, starting transfers between devices: none -> 16.2 us  [the longest x3 9.21 us: attention(): lax.ppermute(mine, 'ctx', [(c, c ^ sharer) for c in range(2 * RING)])]
    all_to_all x0 -> x1, blocking collectives: none -> 14.2 us  [local(): lax.all_to_all(terms.reshape(8, -1, terms.shape[1]), 'tp', 0, 0, tiled=True)]
  transfers between devices with their start and end apart: 5 -> 6, of which waited for: 4 -> 2; matrix products, arithmetic and copies ran while one was open for 5% -> 1% of each run, Pallas kernels for 0% -> 0%
where the time goes in v1:
time: 158 us; the launch traced here: 157 us
  blocking collectives  87.2 us (55%)
  waiting for transfers between devices  29.4 us (19%)
  starting transfers between devices  22.6 us (14%)
  Pallas kernels  11 us (7%)
  local copies, waits for them, and re-layouts  3.83 us (2%)
    all_gather x1, blocking collectives, attention(): lax.all_gather((queries.astype(jnp.float32) * QUERY_SCALE).astype(WIRE),...  39.9 us
    all_gather x1, blocking collectives, local(): lax.all_gather(scaled.astype(WIRE), 'ctx', axis=0, tiled=True, axis_index...  33.2 us
    all_to_all x1, waiting for transfers between devices, attention(): lax.all_to_all(parts, 'ctx', 0, 0, tiled=True, axis_index_groups=EIGHTS)  24.1 us
    all_to_all x1, blocking collectives, local(): lax.all_to_all(terms.reshape(8, -1, terms.shape[1]), 'tp', 0, 0, tiled=True)  14.2 us
    ppermute x3, starting transfers between devices, attention(): lax.ppermute(mine, 'ctx', [(c, c ^ sharer) for c in range(2 * RING)])  9.21 us
    pallas_call x1, Pallas kernels, attend(): pl.pallas_call(functools.partial(attend_kernel, heads, rows, cached, size...  7.17 us
    all_to_all x1, starting transfers between devices, attention(): lax.all_to_all(parts, 'ctx', 0, 0, tiled=True, axis_index_groups=EIGHTS)  6.33 us
    ppermute x1, waiting for transfers between devices, local(): return lax.ppermute(block, ('ctx', 'tp'), home)  5.27 us
  transfers between devices with their start and end apart: 6, of which 2 were waited for; matrix products, arithmetic and copies ran while one was open for 1% of the time, Pallas kernels for 0%

profile of v1, /device:TPU:6, one launch (start us, length us, event | category | flops | bytes accessed | tf_op | source)
XLA Modules:
  0.0 157.0 jit_solution(15696066287482882307)
XLA Ops:
  0.7 0.9 copy-done.1
  1.6 0.9 copy-done.2
  2.5 0.7 copy-done.3
  3.2 0.7 copy-done.4
  3.8 0.4 pack.1.refs_0_
  4.2 4.1 %collective-permute-start.2 = (bf16[1072,128]{1,0:T(8,128)(2,1)S(1)}, bf16[1072,128]{1,0:T(8,128)(2,1)S(1)}, u32[]{:S(2)}, u32[]{:S(2)}) collective-permute-start(bf16[1072,128]{1,0:T(8,128)(2,1)S(1)} %pack.1.refs_0_), channel_id=1, source_target_pairs={{0,272},{16,256},{32,304},{48,288},{64,336},{80,320},{96,368},{112... | collective-permute-start | bytes 823304 | tf_op jit(solution)/shard_map/ppermute | solution.py:246
  8.3 3.1 %collective-permute-start.1 = (bf16[1072,128]{1,0:T(8,128)(2,1)S(1)}, bf16[1072,128]{1,0:T(8,128)(2,1)S(1)}, u32[]{:S(2)}, u32[]{:S(2)}) collective-permute-start(bf16[1072,128]{1,0:T(8,128)(2,1)S(1)} %pack.1.refs_0_), channel_id=1, source_target_pairs={{0,256},{16,272},{32,288},{48,304},{64,320},{80,336},{96,352},{112... | collective-permute-start | bytes 823304 | tf_op jit(solution)/shard_map/ppermute | solution.py:246
  11.4 2.0 %collective-permute-start = (bf16[1072,128]{1,0:T(8,128)(2,1)S(1)}, bf16[1072,128]{1,0:T(8,128)(2,1)}, u32[]{:S(2)}, u32[]{:S(2)}) collective-permute-start(bf16[1072,128]{1,0:T(8,128)(2,1)S(1)} %pack.1.refs_0_), channel_id=1, source_target_pairs={{0,16},{16,0},{32,48},{48,32},{64,80},{80,64},{96,112},{112,96},{1... | collective-permute-start | bytes 823304 | tf_op jit(solution)/shard_map/ppermute | solution.py:246
  13.5 0.9 multiply_convert_fusion.2
  14.3 39.9 %all_gather.6 = f16[128,2048]{1,0:T(8,128)(2,1)S(1)} all-gather(f16[16,2048]{1,0:T(8,128)(2,1)S(1)} %multiply_convert_fusion.2), channel_id=1, replica_groups={{0,32,64,96,128,160,192,224},{16,48,80,112,144,176,208,240},{256,288,32..., dimensions={0}, use_global_device_ids=true | all-gather | bytes 589824 | tf_op jit(solution)/shard_map/all_gather | solution.py:249
  54.2 0.1 multiply_convert_fusion.1.q_ref
  55.0 7.2 %attend.1 = bf16[128,2176]{1,0:T(8,128)(2,1)} custom-call(s32[2]{0:T(128)S(1)} %pad_add_fusion.place_ref, bf16[128,2048]{1,0:T(8,128)(2,1)S(1)} %multiply_convert_fusion.1.q_ref, bf16[1072,128]{1,0:T(8,128)(2,1)S(1)} %pack.1.refs_0_, bf16[1072,128]{1,0:T(8,128)(2,1)} %collective-permute-done.refs_1_, bf16[1072,128]{1,0:T(8,128)(2,1)S(1)} %collective-permute-done.1.refs_2_, ...), custom_call_target="tpu_custom_call" | custom-call | flops 3422552064 | bytes 4194304 | tf_op jit(solution)/shard_map/attend/pallas_call | solution.py:164
  62.2 6.3 %all-to-all-start = ((bf16[8,16,2176]{2,1,0:T(8,128)(2,1)}), bf16[8,16,2176]{2,1,0:T(8,128)(2,1)S(1)}, u32[]{:S(2)}, u32[]{:S(2)}) async-start(bf16[8,16,2176]{2,1,0:T(8,128)(2,1)} %bitcast.2), calls=%async_computation | async-start | bytes 1114112 | tf_op jit(solution)/shard_map/all_to_all | solution.py:256
  68.5 3.0 %collective-permute-start.3 = (bf16[2048,512]{1,0:T(8,128)(2,1)S(1)}, bf16[2048,512]{1,0:T(8,128)(2,1)}, u32[]{:S(2)}, u32[]{:S(2)}) collective-permute-start(bf16[2048,512]{1,0:T(8,128)(2,1)S(1)} %copy-done), channel_id=1, source_target_pairs={{0,256},{16,272},{32,288},{48,304},{64,320},{80,336},{96,352},{112... | collective-permute-start | bytes 6291464 | tf_op jit(solution)/shard_map/ppermute | solution.py:297
  71.6 24.1 %all-to-all-done = bf16[8,16,2176]{2,1,0:T(8,128)(2,1)S(1)} async-done(((bf16[8,16,2176]{2,1,0:T(8,128)(2,1)}), bf16[8,16,2176]{2,1,0:T(8,128)(2,1)S(1)}, u32[]{:S(2)}, u32[]{:S(2)}) %all-to-all-start) | async-done | bytes 557088 | tf_op jit(solution)/shard_map/all_to_all | solution.py:256
  95.7 0.6 merge.1
  96.3 33.2 %all-gather.1 = f16[256,2176]{1,0:T(8,128)(2,1)S(1)} all-gather(f16[16,2176]{1,0:T(8,128)(2,1)S(1)} %convert_element_type.31), channel_id=1, replica_groups={{0,16,32,48,64,80,96,112,128,144,160,176,192,208,224,240},{256,272,288,..., dimensions={0}, use_global_device_ids=true | all-gather | bytes 1183744 | tf_op jit(solution)/shard_map/all_gather | solution.py:298
  129.5 0.1 exponential_reduce_fusion
  129.7 0.3 multiply_convert_fusion.rows_ref
  129.9 2.9 %project.1 = bf16[512,512]{1,0:T(8,128)(2,1)S(1)} custom-call(s32[1]{0:T(128)} %bitcast.place_ref, bf16[256,2048]{1,0:T(8,128)(2,1)S(1)} %multiply_convert_fusion.rows_ref, bf16[2048,512]{1,0:T(8,128)(2,1)S(1)} %copy-done, bf16[2048,512]{1,0:T(8,128)(2,1)} %collective-permute-done.3.their_ref), custom_call_target="tpu_custom_call" | custom-call | flops 1073741824 | bytes 6291456 | tf_op jit(solution)/shard_map/project/pallas_call | solution.py:280
  132.8 14.2 %all_to_all.16 = bf16[8,64,512]{2,1,0:T(8,128)(2,1)S(1)} all-to-all(bf16[8,64,512]{2,1,0:T(8,128)(2,1)S(1)} %bitcast.6), channel_id=1, replica_groups=mesh['ctx'=32,'tp'=8,'rep'=2] {'tp'}, dimensions={0} | all-to-all | bytes 1048576 | tf_op jit(solution)/shard_map/all_to_all | solution.py:303
  147.1 4.0 %collective-permute-start.4 = (f32[64,512]{1,0:T(8,128)S(1)}, f32[64,512]{1,0:T(8,128)S(1)}, u32[]{:S(2)}, u32[]{:S(2)}) collective-permute-start(f32[64,512]{1,0:T(8,128)S(1)} %convert_reduce_fusion), channel_id=1, source_target_pairs={{0,0},{2,2},{4,4},{6,6},{8,256},{10,258},{12,260},{14,262},{16,16}... | collective-permute-start | bytes 393224 | tf_op jit(solution)/shard_map/ppermute | solution.py:311
  151.0 5.3 %collective-permute-done.4 = f32[64,512]{1,0:T(8,128)S(1)} collective-permute-done((f32[64,512]{1,0:T(8,128)S(1)}, f32[64,512]{1,0:T(8,128)S(1)}, u32[]{:S(2)}, u32[]{:S(2)}) %collective-permute-start.4) | collective-permute-done | bytes 131104 | tf_op jit(solution)/shard_map/ppermute | solution.py:311
  156.3 0.7 copy.12
  (13 shorter events, 0.2 us)
Async XLA Ops:
  0.7 0.9 copy-start.1
  1.6 0.9 copy-start.2
  2.5 0.7 copy-start.3
  3.1 0.7 copy-start.4
  4.2 50.8 %collective-permute-start.2 = (bf16[1072,128]{1,0:T(8,128)(2,1)S(1)}, bf16[1072,128]{1,0:T(8,128)(2,1)S(1)}, u32[]{:S(2)}, u32[]{:S(2)}) collective-permute-start(bf16[1072,128]{1,0:T(8,128)(2,1)S(1)} %pack.1.refs_0_), channel_id=1, source_target_pairs={{0,272},{16,256},{32,304},{48,288},{64,336},{80,320},{96,368},{112... | collective-permute-start | bytes 823304 | tf_op jit(solution)/shard_map/ppermute | solution.py:246
  8.3 46.7 %collective-permute-start.1 = (bf16[1072,128]{1,0:T(8,128)(2,1)S(1)}, bf16[1072,128]{1,0:T(8,128)(2,1)S(1)}, u32[]{:S(2)}, u32[]{:S(2)}) collective-permute-start(bf16[1072,128]{1,0:T(8,128)(2,1)S(1)} %pack.1.refs_0_), channel_id=1, source_target_pairs={{0,256},{16,272},{32,288},{48,304},{64,320},{80,336},{96,352},{112... | collective-permute-start | bytes 823304 | tf_op jit(solution)/shard_map/ppermute | solution.py:246
  11.4 43.6 %collective-permute-start = (bf16[1072,128]{1,0:T(8,128)(2,1)S(1)}, bf16[1072,128]{1,0:T(8,128)(2,1)}, u32[]{:S(2)}, u32[]{:S(2)}) collective-permute-start(bf16[1072,128]{1,0:T(8,128)(2,1)S(1)} %pack.1.refs_0_), channel_id=1, source_target_pairs={{0,16},{16,0},{32,48},{48,32},{64,80},{80,64},{96,112},{112,96},{1... | collective-permute-start | bytes 823304 | tf_op jit(solution)/shard_map/ppermute | solution.py:246
  55.0 13.5 %copy-start = (bf16[2048,512]{1,0:T(8,128)(2,1)S(1)}, bf16[2048,512]{1,0:T(8,128)(2,1)}, u32[]{:S(2)}) copy-start(bf16[2048,512]{1,0:T(8,128)(2,1)} %weight_ref.1) | copy-start | bytes 6291460
  62.2 33.5 %all-to-all-start = ((bf16[8,16,2176]{2,1,0:T(8,128)(2,1)}), bf16[8,16,2176]{2,1,0:T(8,128)(2,1)S(1)}, u32[]{:S(2)}, u32[]{:S(2)}) async-start(bf16[8,16,2176]{2,1,0:T(8,128)(2,1)} %bitcast.2), calls=%async_computation | async-start | bytes 1114112 | tf_op jit(solution)/shard_map/all_to_all | solution.py:256
  68.5 61.4 %collective-permute-start.3 = (bf16[2048,512]{1,0:T(8,128)(2,1)S(1)}, bf16[2048,512]{1,0:T(8,128)(2,1)}, u32[]{:S(2)}, u32[]{:S(2)}) collective-permute-start(bf16[2048,512]{1,0:T(8,128)(2,1)S(1)} %copy-done), channel_id=1, source_target_pairs={{0,256},{16,272},{32,288},{48,304},{64,320},{80,336},{96,352},{112... | collective-permute-start | bytes 6291464 | tf_op jit(solution)/shard_map/ppermute | solution.py:297
  147.1 9.3 %collective-permute-start.4 = (f32[64,512]{1,0:T(8,128)S(1)}, f32[64,512]{1,0:T(8,128)S(1)}, u32[]{:S(2)}, u32[]{:S(2)}) collective-permute-start(f32[64,512]{1,0:T(8,128)S(1)} %convert_reduce_fusion), channel_id=1, source_target_pairs={{0,0},{2,2},{4,4},{6,6},{8,256},{10,258},{12,260},{14,262},{16,16}... | collective-permute-start | bytes 393224 | tf_op jit(solution)/shard_map/ppermute | solution.py:311

commit v2 on v1

--- a/solution.py
+++ b/solution.py
@@ -17,9 +17,14 @@
 VMEM_LIMIT = 48 * 1024 * 1024
 
 
-SHARERS = (0, 1, RING, RING + 1)
+SHARED = ((0, 0), (1, 0), (0, 1), (1, 1))
 ACROSS = [(c, c ^ RING) for c in range(2 * RING)]
 EIGHTS = [[x * RING + p + 2 * i for i in range(RING // 2)] for x in range(2) for p in range(2)]
+PAIRS_OF_CORES = [
+    [(x * RING + z) * 8 + 2 * y + core for x in range(2) for core in range(2)]
+    for z in range(RING)
+    for y in range(4)
+]
 RINGS = [[x * RING + z for z in range(RING)] for x in range(2)]
 WIRE = jnp.float16
 QUERY_SCALE = 4096.0
@@ -35,18 +40,18 @@
 
 def pack_kernel(length_ref, k_ref, nk_ref, v_ref, nv_ref, o_ref, sems):
     cached, rows = k_ref.shape[0], nk_ref.shape[0]
+    total = 2 * (cached + rows)
+    size = total + 16
     copies, start = [], 0
     for i, ref in enumerate((k_ref, nk_ref, v_ref, nv_ref)):
-        size = ref.shape[0]
-        copies.append(
-            pltpu.make_async_copy(ref, o_ref.at[pl.ds(start, size)], sems.at[i])
-        )
+        count = ref.shape[0]
+        copies.append(pltpu.make_async_copy(ref, o_ref.at[pl.ds(start, count)], sems.at[i]))
         copies[-1].start()
-        start += size
+        start += count
     row = lax.broadcasted_iota(jnp.int32, (16, LANES), 0)
     filled = length_ref[0]
     digit = jnp.where(row < 8, filled // 16, filled % 16)
-    o_ref[2 * (cached + rows) :] = digit.astype(jnp.float32).astype(jnp.bfloat16)
+    o_ref[total:size] = digit.astype(jnp.float32).astype(jnp.bfloat16)
     for copy in copies:
         copy.wait()
 
@@ -60,17 +65,17 @@
         + [pl.BlockSpec(memory_space=pltpu.HBM)] * 4,
         out_specs=pl.BlockSpec(memory_space=pltpu.VMEM),
         scratch_shapes=[pltpu.SemaphoreType.DMA((4,))],
-        compiler_params=PARAMS,
+        compiler_params=pltpu.CompilerParams(vmem_limit_bytes=60 * 1024 * 1024),
         name="pack",
     )(length, k, nk, v, nv)
 
 
 def attend_kernel(heads, rows, cached, sizes, place_ref, q_ref, *refs):
-    kv_refs = refs[: len(SHARERS)]
-    o_ref, k_all, v_all = refs[len(SHARERS) :]
+    kv_refs = refs[: len(SHARED)]
+    o_ref, k_all, v_all = refs[len(SHARED) :]
     begin, me = place_ref[0], place_ref[1]
     span = cached + rows
-    fresh = len(SHARERS) * rows
+    fresh = len(SHARED) * rows
     cycle = 2 * RING
     keys = k_all.shape[0]
 
@@ -81,8 +86,9 @@
     new_pos = jnp.full((1, LANES), far_away, jnp.int32)
     starts, ends = [], []
     end = fresh
-    for i, (sharer, ref) in enumerate(zip(SHARERS, kv_refs)):
-        index = jnp.bitwise_xor(me, sharer)
+    x, z = me // RING, me % RING
+    for i, ((dx, dz), ref) in enumerate(zip(SHARED, kv_refs)):
+        index = lax.rem(x + dx, 2) * RING + lax.rem(z + dz, RING)
         at = slice(i * rows, (i + 1) * rows)
         k_all[at] = ref[cached:span]
         v_all[at, :HEAD_SIZE] = ref[span + cached : 2 * span]
@@ -101,7 +107,7 @@
 
     token = lax.broadcasted_iota(jnp.int32, (heads * rows, LANES), 0) % rows
     lanes = lax.broadcasted_iota(jnp.int32, (rows, LANES), 1)
-    parity, x = me % 2, me // RING
+    parity = me % 2
 
     def run(size):
         slot = lax.broadcasted_iota(jnp.int32, (1, size), 1)
@@ -159,7 +165,7 @@
     count, width = gathered.shape
     heads = width // HEAD_SIZE
     cached = (blocks[0].shape[0] - 16) // 2 - rows
-    most = -(-len(blocks) * (cached + rows) // LANES) * LANES
+    most = -(-len(SHARED) * (cached + rows) // LANES) * LANES
     sizes = tuple(-(-most * i // 4 // LANES) * LANES for i in (1, 2, 3, 4))
     return pl.pallas_call(
         functools.partial(attend_kernel, heads, rows, cached, sizes),
@@ -243,8 +249,16 @@
     rows = queries.shape[0]
     mine = pack(cache_lengths, cache_k, new_token_keys, cached_values, new_token_values)
     blocks = [mine] + [
-        lax.ppermute(mine, "ctx", [(c, c ^ sharer) for c in range(2 * RING)])
-        for sharer in SHARERS[1:]
+        lax.ppermute(
+            mine,
+            "ctx",
+            [
+                ((x + dx) % 2 * RING + (z + dz) % RING, x * RING + z)
+                for x in range(2)
+                for z in range(RING)
+            ],
+        )
+        for dx, dz in SHARED[1:]
     ]
     gathered = lax.all_gather(
         (queries.astype(jnp.float32) * QUERY_SCALE).astype(WIRE),
@@ -267,11 +281,16 @@
 def project_kernel(place_ref, rows_ref, weight_ref, their_ref, o_ref):
     x = place_ref[0]
     height = rows_ref.shape[0]
+    chunk = height // 4
     for ref, column in ((weight_ref, x), (their_ref, 1 - x)):
-        at = pl.ds(pl.multiple_of(column * height, height), height)
-        o_ref[at, :] = jnp.dot(
+        product = jnp.dot(
             rows_ref[...], ref[...], preferred_element_type=jnp.float32
         ).astype(jnp.bfloat16)
+        for i in range(4):
+            to = column * height + ((i % 2) * 2 + i // 2) * chunk
+            o_ref[pl.ds(pl.multiple_of(to, chunk), chunk), :] = product[
+                i * chunk : (i + 1) * chunk
+            ]
 
 
 def project(x, rows, weight, theirs):
@@ -298,17 +317,17 @@
     scaled = lax.all_gather(
         scaled.astype(WIRE), "ctx", axis=0, tiled=True, axis_index_groups=RINGS
     )
-    x = (lax.axis_index("ctx") // RING).astype(jnp.int32).reshape(1)
-    terms = project(x, attended_rows(scaled), out_weight, their_weight)
-    terms = lax.all_to_all(terms.reshape(8, -1, terms.shape[1]), "tp", 0, 0, tiled=True)
-    block = jnp.sum(terms.astype(jnp.float32), axis=0)
-    home = [
-        ((x * RING + z) * 8 + j, ((j // 4) * RING + z) * 8 + 4 * x + j % 4)
-        for x in range(2)
-        for z in range(RING)
-        for j in range(8)
-    ]
-    return lax.ppermute(block, ("ctx", "tp"), home)
+    rows = attended_rows(scaled)
+    x = (lax.axis_index("ctx") // RING).astype(jnp.int32)
+    terms = project(x.reshape(1), rows, out_weight, their_weight)
+    terms = lax.all_to_all(
+        terms, ("ctx", "tp"), 0, 0, tiled=True, axis_index_groups=PAIRS_OF_CORES
+    )
+    terms = terms.reshape(2, 2, -1, terms.shape[1]).astype(jnp.float32)
+    terms = jnp.sum(terms, axis=1).astype(jnp.bfloat16)
+    terms = terms.reshape(-1, terms.shape[2])
+    terms = lax.all_to_all(terms, "tp", 0, 0, tiled=True, axis_index_groups=[[0, 2, 4, 6], [1, 3, 5, 7]])
+    return jnp.sum(terms.reshape(4, -1, terms.shape[1]).astype(jnp.float32), axis=0)
 
 
 def solution(mesh):

time: 158 us -> 155 us (0.981)
  waiting for transfers between devices: 29.4 us -> 21.5 us
  starting transfers between devices: 22.6 us -> 29 us
  local copies, waits for them, and re-layouts: 3.83 us -> 1.1 us
    all_gather x1, blocking collectives: 39.9 us -> 30.2 us  [attention(): lax.all_gather((queries.astype(jnp.float32) * QUERY_SCALE).astype(WIRE),...]
    all_to_all x1 -> x2, blocking collectives: 14.2 us -> 22.8 us  [the longest x1 11.8 us: local(): lax.all_to_all(terms, ('ctx', 'tp'), 0, 0, tiled=True, axis_index_groups=...]
    ppermute x4 -> x3, waiting for transfers between devices: 5.28 us -> 0.01 us  [attention(): lax.ppermute(mine, 'ctx', [((x + dx) % 2 * RING + (z + dz) % RING, x * RI...]
    ppermute x4 -> x3, starting transfers between devices: 13.2 us -> 17.7 us  [attention(): lax.ppermute(mine, 'ctx', [((x + dx) % 2 * RING + (z + dz) % RING, x * RI...]
    unnamed x11 -> x4, local copies, waits for them, and re-layouts: 3.83 us -> 1.1 us
    all_to_all x1, waiting for transfers between devices: 24.1 us -> 21.5 us  [attention(): lax.all_to_all(parts, 'ctx', 0, 0, tiled=True, axis_index_groups=EIGHTS)]
    pallas_call x1, Pallas kernels: 7.17 us -> 5.12 us  [attend(): pl.pallas_call(functools.partial(attend_kernel, heads, rows, cached, size...]
    all_to_all x1, starting transfers between devices: 6.33 us -> 8.09 us  [attention(): lax.all_to_all(parts, 'ctx', 0, 0, tiled=True, axis_index_groups=EIGHTS)]
  transfers between devices with their start and end apart: 6 -> 5, of which waited for: 2 -> 1; matrix products, arithmetic and copies ran while one was open for 1% -> 1% of each run, Pallas kernels for 0% -> 0%
where the time goes in v2:
time: 155 us; the launch traced here: 153 us
  blocking collectives  87.4 us (56%)
  starting transfers between devices  29 us (19%)
  waiting for transfers between devices  21.5 us (14%)
  Pallas kernels  10.3 us (7%)
  other arithmetic  2.18 us (1%)
    all_gather x1, blocking collectives, local(): lax.all_gather(scaled.astype(WIRE), 'ctx', axis=0, tiled=True, axis_index...  34.4 us
    all_gather x1, blocking collectives, attention(): lax.all_gather((queries.astype(jnp.float32) * QUERY_SCALE).astype(WIRE),...  30.2 us
    all_to_all x1, waiting for transfers between devices, attention(): lax.all_to_all(parts, 'ctx', 0, 0, tiled=True, axis_index_groups=EIGHTS)  21.5 us
    ppermute x3, starting transfers between devices, attention(): lax.ppermute(mine, 'ctx', [((x + dx) % 2 * RING + (z + dz) % RING, x * RI...  17.7 us
    all_to_all x1, blocking collectives, local(): lax.all_to_all(terms, ('ctx', 'tp'), 0, 0, tiled=True, axis_index_groups=...  11.8 us
    all_to_all x1, blocking collectives, local(): lax.all_to_all(terms, 'tp', 0, 0, tiled=True, axis_index_groups=[[0, 2, 4...  11 us
    all_to_all x1, starting transfers between devices, attention(): lax.all_to_all(parts, 'ctx', 0, 0, tiled=True, axis_index_groups=EIGHTS)  8.09 us
    pallas_call x1, Pallas kernels, attend(): pl.pallas_call(functools.partial(attend_kernel, heads, rows, cached, size...  5.12 us
  transfers between devices with their start and end apart: 5, of which 1 were waited for; matrix products, arithmetic and copies ran while one was open for 1% of the time, Pallas kernels for 0%

profile of v2, /device:TPU:6, one launch (start us, length us, event | category | flops | bytes accessed | tf_op | source)
XLA Modules:
  0.0 152.8 jit_solution(3593182262474708550)
XLA Ops:
  0.7 1.7 %pack.1.refs_0_ = bf16[1072,128]{1,0:T(8,128)(2,1)} custom-call(s32[1]{0:T(128)S(6)} %copy.9.length_ref, bf16[512,128]{1,0:T(8,128)(2,1)} %k_ref.1, bf16[16,128]{1,0:T(8,128)(2,1)} %nk_ref.1, bf16[512,128]{1,0:T(8,128)(2,1)} %v_ref.1, bf16[16,128]{1,0:T(8,128)(2,1)} %nv_ref.1), custom_call_target="tpu_custom_call" | custom-call | tf_op jit(solution)/shard_map/pack/pallas_call | solution.py:61
  2.4 11.7 %collective-permute-start.2 = (bf16[1072,128]{1,0:T(8,128)(2,1)}, bf16[1072,128]{1,0:T(8,128)(2,1)S(1)}, u32[]{:S(2)}, u32[]{:S(2)}) collective-permute-start(bf16[1072,128]{1,0:T(8,128)(2,1)} %pack.1.refs_0_), channel_id=1, source_target_pairs={{272,0},{288,16},{304,32},{320,48},{336,64},{352,80},{368,96},{384... | collective-permute-start | bytes 823304 | tf_op jit(solution)/shard_map/ppermute | solution.py:252
  14.1 2.9 %collective-permute-start.1 = (bf16[1072,128]{1,0:T(8,128)(2,1)}, bf16[1072,128]{1,0:T(8,128)(2,1)S(1)}, u32[]{:S(2)}, u32[]{:S(2)}) collective-permute-start(bf16[1072,128]{1,0:T(8,128)(2,1)} %pack.1.refs_0_), channel_id=1, source_target_pairs={{16,0},{32,16},{48,32},{64,48},{80,64},{96,80},{112,96},{128,112},... | collective-permute-start | bytes 823304 | tf_op jit(solution)/shard_map/ppermute | solution.py:252
  17.0 3.1 %collective-permute-start = (bf16[1072,128]{1,0:T(8,128)(2,1)}, bf16[1072,128]{1,0:T(8,128)(2,1)S(1)}, u32[]{:S(2)}, u32[]{:S(2)}) collective-permute-start(bf16[1072,128]{1,0:T(8,128)(2,1)} %pack.1.refs_0_), channel_id=1, source_target_pairs={{256,0},{272,16},{288,32},{304,48},{320,64},{336,80},{352,96},{368... | collective-permute-start | bytes 823304 | tf_op jit(solution)/shard_map/ppermute | solution.py:252
  20.1 0.9 multiply_convert_fusion.2
  21.0 30.2 %all_gather.6 = f16[128,2048]{1,0:T(8,128)(2,1)S(1)} all-gather(f16[16,2048]{1,0:T(8,128)(2,1)S(1)} %multiply_convert_fusion.2), channel_id=1, replica_groups={{0,32,64,96,128,160,192,224},{16,48,80,112,144,176,208,240},{256,288,32..., dimensions={0}, use_global_device_ids=true | all-gather | bytes 589824 | tf_op jit(solution)/shard_map/all_gather | solution.py:263
  51.2 0.1 multiply_convert_fusion.1.q_ref
  51.9 0.1 pad_add_fusion.place_ref
  52.0 0.0 collective-permute-done.2.refs_3_
  52.0 0.0 collective-permute-done.1.refs_2_
  52.0 1.1 copy-done.1
  53.1 5.1 %attend.1 = bf16[128,2176]{1,0:T(8,128)(2,1)} custom-call(s32[2]{0:T(128)S(1)} %pad_add_fusion.place_ref, bf16[128,2048]{1,0:T(8,128)(2,1)S(1)} %multiply_convert_fusion.1.q_ref, bf16[1072,128]{1,0:T(8,128)(2,1)S(1)} %copy-done.1, bf16[1072,128]{1,0:T(8,128)(2,1)S(1)} %collective-permute-done.refs_1_, bf16[1072,128]{1,0:T(8,128)(2,1)S(1)} %collective-permute-done.1.refs_2_, ...), custom_call_target="tpu_custom_call" | custom-call | flops 3422552064 | bytes 4194304 | tf_op jit(solution)/shard_map/attend/pallas_call | solution.py:170
  58.2 8.1 %all-to-all-start = ((bf16[8,16,2176]{2,1,0:T(8,128)(2,1)}), bf16[8,16,2176]{2,1,0:T(8,128)(2,1)S(1)}, u32[]{:S(2)}, u32[]{:S(2)}) async-start(bf16[8,16,2176]{2,1,0:T(8,128)(2,1)} %bitcast.2), calls=%async_computation | async-start | bytes 1114112 | tf_op jit(solution)/shard_map/all_to_all | solution.py:270
  66.3 3.2 %collective-permute-start.3 = (bf16[2048,512]{1,0:T(8,128)(2,1)S(1)}, bf16[2048,512]{1,0:T(8,128)(2,1)}, u32[]{:S(2)}, u32[]{:S(2)}) collective-permute-start(bf16[2048,512]{1,0:T(8,128)(2,1)S(1)} %copy-done), channel_id=1, source_target_pairs={{0,256},{16,272},{32,288},{48,304},{64,320},{80,336},{96,352},{112... | collective-permute-start | bytes 6291464 | tf_op jit(solution)/shard_map/ppermute | solution.py:316
  69.5 21.5 %all-to-all-done = bf16[8,16,2176]{2,1,0:T(8,128)(2,1)S(1)} async-done(((bf16[8,16,2176]{2,1,0:T(8,128)(2,1)}), bf16[8,16,2176]{2,1,0:T(8,128)(2,1)S(1)}, u32[]{:S(2)}, u32[]{:S(2)}) %all-to-all-start) | async-done | bytes 557088 | tf_op jit(solution)/shard_map/all_to_all | solution.py:270
  91.0 0.6 merge.1
  91.6 34.4 %all-gather.1 = f16[256,2176]{1,0:T(8,128)(2,1)S(1)} all-gather(f16[16,2176]{1,0:T(8,128)(2,1)S(1)} %convert_element_type.33), channel_id=1, replica_groups={{0,16,32,48,64,80,96,112,128,144,160,176,192,208,224,240},{256,272,288,..., dimensions={0}, use_global_device_ids=true | all-gather | bytes 1183744 | tf_op jit(solution)/shard_map/all_gather | solution.py:317
  126.0 0.1 exponential_reduce_fusion
  126.1 0.3 multiply_convert_fusion.rows_ref
  126.4 2.8 %project.1 = bf16[512,512]{1,0:T(8,128)(2,1)S(1)} custom-call(s32[1]{0:T(128)} %bitcast.place_ref, bf16[256,2048]{1,0:T(8,128)(2,1)S(1)} %multiply_convert_fusion.rows_ref, bf16[2048,512]{1,0:T(8,128)(2,1)S(1)} %copy-done, bf16[2048,512]{1,0:T(8,128)(2,1)} %collective-permute-done.3.their_ref), custom_call_target="tpu_custom_call" | custom-call | flops 1073741824 | bytes 6291456 | tf_op jit(solution)/shard_map/project/pallas_call | solution.py:299
  129.3 11.8 %all_to_all.29 = bf16[4,128,512]{2,1,0:T(8,128)(2,1)S(1)} all-to-all(bf16[4,128,512]{2,1,0:T(8,128)(2,1)S(1)} %bitcast.9), channel_id=1, replica_groups={{0,2,256,258},{4,6,260,262},{8,10,264,266},{12,14,268,270},{16,18,272,2..., dimensions={0} | all-to-all | bytes 1048576 | tf_op jit(solution)/shard_map/all_to_all | solution.py:323
  141.1 0.1 bitcast_reduce_fusion
  141.1 11.0 %all_to_all.30 = bf16[4,64,512]{2,1,0:T(8,128)(2,1)S(1)} all-to-all(bf16[4,64,512]{2,1,0:T(8,128)(2,1)S(1)} %bitcast.10), channel_id=1, replica_groups={{0,4,8,12},{2,6,10,14},{1,5,9,13},{3,7,11,15},{16,20,24,28},{18,22,26,3..., dimensions={0} | all-to-all | bytes 524288 | tf_op jit(solution)/shard_map/all_to_all | solution.py:329
  152.1 0.7 convert_reduce_fusion
  (6 shorter events, 0.0 us)
Async XLA Ops:
  2.4 49.6 %collective-permute-start.2 = (bf16[1072,128]{1,0:T(8,128)(2,1)}, bf16[1072,128]{1,0:T(8,128)(2,1)S(1)}, u32[]{:S(2)}, u32[]{:S(2)}) collective-permute-start(bf16[1072,128]{1,0:T(8,128)(2,1)} %pack.1.refs_0_), channel_id=1, source_target_pairs={{272,0},{288,16},{304,32},{320,48},{336,64},{352,80},{368,96},{384... | collective-permute-start | bytes 823304 | tf_op jit(solution)/shard_map/ppermute | solution.py:252
  14.1 37.9 %collective-permute-start.1 = (bf16[1072,128]{1,0:T(8,128)(2,1)}, bf16[1072,128]{1,0:T(8,128)(2,1)S(1)}, u32[]{:S(2)}, u32[]{:S(2)}) collective-permute-start(bf16[1072,128]{1,0:T(8,128)(2,1)} %pack.1.refs_0_), channel_id=1, source_target_pairs={{16,0},{32,16},{48,32},{64,48},{80,64},{96,80},{112,96},{128,112},... | collective-permute-start | bytes 823304 | tf_op jit(solution)/shard_map/ppermute | solution.py:252
  17.0 35.0 %collective-permute-start = (bf16[1072,128]{1,0:T(8,128)(2,1)}, bf16[1072,128]{1,0:T(8,128)(2,1)S(1)}, u32[]{:S(2)}, u32[]{:S(2)}) collective-permute-start(bf16[1072,128]{1,0:T(8,128)(2,1)} %pack.1.refs_0_), channel_id=1, source_target_pairs={{256,0},{272,16},{288,32},{304,48},{320,64},{336,80},{352,96},{368... | collective-permute-start | bytes 823304 | tf_op jit(solution)/shard_map/ppermute | solution.py:252
  52.0 14.3 %copy-start = (bf16[2048,512]{1,0:T(8,128)(2,1)S(1)}, bf16[2048,512]{1,0:T(8,128)(2,1)}, u32[]{:S(2)}) copy-start(bf16[2048,512]{1,0:T(8,128)(2,1)} %weight_ref.1) | copy-start | bytes 6291460
  52.0 1.1 copy-start.1
  58.2 32.8 %all-to-all-start = ((bf16[8,16,2176]{2,1,0:T(8,128)(2,1)}), bf16[8,16,2176]{2,1,0:T(8,128)(2,1)S(1)}, u32[]{:S(2)}, u32[]{:S(2)}) async-start(bf16[8,16,2176]{2,1,0:T(8,128)(2,1)} %bitcast.2), calls=%async_computation | async-start | bytes 1114112 | tf_op jit(solution)/shard_map/all_to_all | solution.py:270
  66.3 60.1 %collective-permute-start.3 = (bf16[2048,512]{1,0:T(8,128)(2,1)S(1)}, bf16[2048,512]{1,0:T(8,128)(2,1)}, u32[]{:S(2)}, u32[]{:S(2)}) collective-permute-start(bf16[2048,512]{1,0:T(8,128)(2,1)S(1)} %copy-done), channel_id=1, source_target_pairs={{0,256},{16,272},{32,288},{48,304},{64,320},{80,336},{96,352},{112... | collective-permute-start | bytes 6291464 | tf_op jit(solution)/shard_map/ppermute | solution.py:316

commit v3 on v2

--- a/solution.py
+++ b/solution.py
@@ -14,7 +14,7 @@
 very_low = -1e30
 far_away = 1073741824
 FACTOR = float(HEAD_SIZE ** (-0.5) * np.log2(np.e))
-VMEM_LIMIT = 48 * 1024 * 1024
+VMEM_LIMIT = 32 * 1024 * 1024
 
 
 SHARED = ((0, 0), (1, 0), (0, 1), (1, 1))
@@ -27,6 +27,7 @@
 ]
 RINGS = [[x * RING + z for z in range(RING)] for x in range(2)]
 WIRE = jnp.float16
+POWER_LANE = 96
 QUERY_SCALE = 4096.0
 ROW_TOP = 13
 
@@ -84,7 +85,8 @@
     v_all[:, HEAD_SIZE:] = jnp.ones((keys, HEAD_SIZE), jnp.bfloat16)
     lane = lax.broadcasted_iota(jnp.int32, (1, LANES), 1)
     new_pos = jnp.full((1, LANES), far_away, jnp.int32)
-    starts, ends = [], []
+    row = lax.broadcasted_iota(jnp.int32, (cached, HEAD_SIZE), 0)
+    starts, ends, live_values = [], [], []
     end = fresh
     x, z = me // RING, me % RING
     for i, ((dx, dz), ref) in enumerate(zip(SHARED, kv_refs)):
@@ -101,9 +103,18 @@
         to = pl.ds(pl.multiple_of(end, 16), cached)
         k_all[to, :] = ref[:cached]
         v_all[to, :HEAD_SIZE] = ref[span : span + cached]
+        values = jnp.abs(ref[span : span + cached].astype(jnp.float32))
+        live_values.append(jnp.where(row < live, values, 0.0))
+        live_values.append(jnp.abs(ref[span + cached : 2 * span].astype(jnp.float32)))
         starts.append(end)
         ends.append(end + live)
         end = end + (live + 15) // 16 * 16
+
+    largest = functools.reduce(
+        jnp.maximum, [jnp.max(part, axis=0, keepdims=True) for part in live_values]
+    )
+    largest = jnp.max(largest, axis=1, keepdims=True)
+    power = jnp.ceil(jnp.log2(jnp.maximum(largest, 1e-30)))
 
     token = lax.broadcasted_iota(jnp.int32, (heads * rows, LANES), 0) % rows
     lanes = lax.broadcasted_iota(jnp.int32, (rows, LANES), 1)
@@ -148,7 +159,9 @@
                 part = slice(h * rows, (h + 1) * rows)
                 o_ref[at, h * HEAD_SIZE : (h + 1) * HEAD_SIZE] = value[part].astype(jnp.bfloat16)
                 packed = jnp.where(lanes == h, level[part], packed)
-            o_ref[at, heads * HEAD_SIZE :] = pack_level(packed)
+            o_ref[at, heads * HEAD_SIZE :] = jnp.where(
+                lanes == POWER_LANE, power, pack_level(packed).astype(jnp.float32)
+            ).astype(jnp.bfloat16)
 
         @pl.loop(0, RING // 4)
         def _(pair):
@@ -166,7 +179,7 @@
     heads = width // HEAD_SIZE
     cached = (blocks[0].shape[0] - 16) // 2 - rows
     most = -(-len(SHARED) * (cached + rows) // LANES) * LANES
-    sizes = tuple(-(-most * i // 4 // LANES) * LANES for i in (1, 2, 3, 4))
+    sizes = tuple(-(-most * i // (8 * LANES)) * LANES for i in range(1, 9))
     return pl.pallas_call(
         functools.partial(attend_kernel, heads, rows, cached, sizes),
         out_shape=jax.ShapeDtypeStruct((count, width + LANES), jnp.bfloat16),
@@ -199,27 +212,25 @@
     return spread + pltpu.roll(spread, 96, 1) + pltpu.roll(spread, 64, 1)
 
 
-def merge_kernel(rows, heads, parts_ref, o_ref, value_ref):
-    lane = lax.broadcasted_iota(jnp.int32, (rows, LANES), 1)
+def merge_kernel(rows, heads, parts_ref, o_ref, power_ref):
     parts = [slice(i * rows, (i + 1) * rows) for i in range(parts_ref.shape[0] // rows)]
-    levels = [unpack_level(parts_ref[at, heads * HEAD_SIZE :]) for at in parts]
+    tails = [parts_ref[at, heads * HEAD_SIZE :] for at in parts]
+    levels = [unpack_level(tail) for tail in tails]
+    power = functools.reduce(
+        jnp.maximum,
+        [tail.astype(jnp.float32)[:, POWER_LANE : POWER_LANE + 1] for tail in tails],
+    )
     top = functools.reduce(jnp.maximum, levels)
     weights = [jnp.exp2(level - top) for level in levels]
-    total = 1 / sum(weights)
+    total = jnp.exp2(ROW_TOP - power) / sum(weights)
     scales = [weight * total for weight in weights]
-    largest = jnp.zeros((rows, HEAD_SIZE), jnp.float32)
     for h in range(heads):
         span = slice(h * HEAD_SIZE, (h + 1) * HEAD_SIZE)
-        value = sum(
+        o_ref[:, span] = sum(
             parts_ref[at, span].astype(jnp.float32) * scale[:, h : h + 1]
             for at, scale in zip(parts, scales)
         )
-        value_ref[:, span] = value
-        largest = jnp.maximum(largest, jnp.abs(value))
-    largest = jnp.max(largest, axis=1, keepdims=True)
-    power = jnp.floor(jnp.log2(jnp.maximum(largest, 1e-30)))
-    o_ref[:, : heads * HEAD_SIZE] = value_ref[...] * jnp.exp2(ROW_TOP - power)
-    o_ref[:, heads * HEAD_SIZE :] = jnp.where(lane >= 0, power, 0.0)
+    power_ref[...] = jnp.broadcast_to(power, power_ref.shape)
 
 
 def merge(parts, rows):
@@ -227,11 +238,13 @@
     heads = width // HEAD_SIZE - 1
     return pl.pallas_call(
         functools.partial(merge_kernel, rows, heads),
-        out_shape=jax.ShapeDtypeStruct((rows, width), jnp.float32),
+        out_shape=[
+            jax.ShapeDtypeStruct((rows, heads * HEAD_SIZE), jnp.float32),
+            jax.ShapeDtypeStruct((rows, LANES), jnp.float32),
+        ],
         in_specs=vmem_specs(1),
-        out_specs=pl.BlockSpec(memory_space=pltpu.VMEM),
-        scratch_shapes=[pltpu.VMEM((rows, heads * HEAD_SIZE), jnp.float32)],
-        compiler_params=PARAMS,
+        out_specs=vmem_specs(2),
+        compiler_params=pltpu.CompilerParams(vmem_limit_bytes=16 * 1024 * 1024),
         name="merge",
     )(parts)
 
@@ -271,21 +284,14 @@
     return merge(parts, rows), gathered
 
 
-def attended_rows(scaled):
-    rows = scaled[:, :-LANES].astype(jnp.float32) * jnp.exp2(
-        scaled[:, -LANES : 1 - LANES].astype(jnp.float32) - ROW_TOP
-    )
-    return rows.astype(jnp.bfloat16)
-
-
-def project_kernel(place_ref, rows_ref, weight_ref, their_ref, o_ref):
+def project_kernel(place_ref, power_ref, rows_ref, weight_ref, their_ref, o_ref):
     x = place_ref[0]
     height = rows_ref.shape[0]
     chunk = height // 4
+    scale = jnp.exp2(power_ref[:1, :1] - ROW_TOP)
     for ref, column in ((weight_ref, x), (their_ref, 1 - x)):
-        product = jnp.dot(
-            rows_ref[...], ref[...], preferred_element_type=jnp.float32
-        ).astype(jnp.bfloat16)
+        product = jnp.dot(rows_ref[...], ref[...], preferred_element_type=jnp.float32)
+        product = (product * scale).astype(jnp.bfloat16)
         for i in range(4):
             to = column * height + ((i % 2) * 2 + i // 2) * chunk
             o_ref[pl.ds(pl.multiple_of(to, chunk), chunk), :] = product[
@@ -293,33 +299,34 @@
             ]
 
 
-def project(x, rows, weight, theirs):
+def project(x, power, rows, weight, theirs):
     height, depth = rows.shape
     width = weight.shape[1]
     return pl.pallas_call(
         project_kernel,
         out_shape=jax.ShapeDtypeStruct((2 * height, width), jnp.bfloat16),
-        in_specs=[pl.BlockSpec(memory_space=pltpu.SMEM)] + vmem_specs(3),
+        in_specs=[pl.BlockSpec(memory_space=pltpu.SMEM)] + vmem_specs(4),
         out_specs=pl.BlockSpec(memory_space=pltpu.VMEM),
         compiler_params=PARAMS,
         cost_estimate=pl.CostEstimate(
             flops=4 * height * depth * width, bytes_accessed=6 << 20, transcendentals=0
         ),
         name="project",
-    )(x, rows, weight, theirs)
+    )(x, power, rows, weight, theirs)
 
 
 def local(*arguments):
     out_weight = arguments[-1]
-    scaled, first = attention(*arguments[:-1])
+    (scaled, power), first = attention(*arguments[:-1])
     their_weight, _ = lax.optimization_barrier((out_weight, first))
     their_weight = lax.ppermute(their_weight, "ctx", ACROSS)
     scaled = lax.all_gather(
         scaled.astype(WIRE), "ctx", axis=0, tiled=True, axis_index_groups=RINGS
     )
-    rows = attended_rows(scaled)
     x = (lax.axis_index("ctx") // RING).astype(jnp.int32)
-    terms = project(x.reshape(1), rows, out_weight, their_weight)
+    terms = project(
+        x.reshape(1), power, scaled.astype(jnp.bfloat16), out_weight, their_weight
+    )
     terms = lax.all_to_all(
         terms, ("ctx", "tp"), 0, 0, tiled=True, axis_index_groups=PAIRS_OF_CORES
     )

time: 155 us -> 154 us (level)
  no operation moved by 1% of the time
where the time goes in v3:
time: 154 us; the launch traced here: 152 us
  blocking collectives  86.9 us (56%)
  starting transfers between devices  29 us (19%)
  waiting for transfers between devices  21.5 us (14%)
  Pallas kernels  10.5 us (7%)
  other arithmetic  2 us (1%)
    all_gather x1, blocking collectives, local(): lax.all_gather(scaled.astype(WIRE), 'ctx', axis=0, tiled=True, axis_index...  34 us
    all_gather x1, blocking collectives, attention(): lax.all_gather((queries.astype(jnp.float32) * QUERY_SCALE).astype(WIRE),...  30.2 us
    all_to_all x1, waiting for transfers between devices, attention(): lax.all_to_all(parts, 'ctx', 0, 0, tiled=True, axis_index_groups=EIGHTS)  21.5 us
    ppermute x3, starting transfers between devices, attention(): lax.ppermute(mine, 'ctx', [((x + dx) % 2 * RING + (z + dz) % RING, x * RI...  17.7 us
    all_to_all x1, blocking collectives, local(): lax.all_to_all(terms, ('ctx', 'tp'), 0, 0, tiled=True, axis_index_groups=...  11.7 us
    all_to_all x1, blocking collectives, local(): lax.all_to_all(terms, 'tp', 0, 0, tiled=True, axis_index_groups=[[0, 2, 4...  11 us
    all_to_all x1, starting transfers between devices, attention(): lax.all_to_all(parts, 'ctx', 0, 0, tiled=True, axis_index_groups=EIGHTS)  8.09 us
    pallas_call x1, Pallas kernels, attend(): pl.pallas_call(functools.partial(attend_kernel, heads, rows, cached, size...  5.45 us
  transfers between devices with their start and end apart: 5, of which 1 were waited for; matrix products, arithmetic and copies ran while one was open for 1% of the time, Pallas kernels for 0%

profile of v3, /device:TPU:6, one launch (start us, length us, event | category | flops | bytes accessed | tf_op | source)
XLA Modules:
  0.0 152.4 jit_solution(15762776902976755688)
XLA Ops:
  0.7 1.7 %pack.1.refs_0_ = bf16[1072,128]{1,0:T(8,128)(2,1)} custom-call(s32[1]{0:T(128)S(6)} %copy.9.length_ref, bf16[512,128]{1,0:T(8,128)(2,1)} %k_ref.1, bf16[16,128]{1,0:T(8,128)(2,1)} %nk_ref.1, bf16[512,128]{1,0:T(8,128)(2,1)} %v_ref.1, bf16[16,128]{1,0:T(8,128)(2,1)} %nv_ref.1), custom_call_target="tpu_custom_call" | custom-call | tf_op jit(solution)/shard_map/pack/pallas_call | solution.py:62
  2.4 11.7 %collective-permute-start.2 = (bf16[1072,128]{1,0:T(8,128)(2,1)}, bf16[1072,128]{1,0:T(8,128)(2,1)S(1)}, u32[]{:S(2)}, u32[]{:S(2)}) collective-permute-start(bf16[1072,128]{1,0:T(8,128)(2,1)} %pack.1.refs_0_), channel_id=1, source_target_pairs={{272,0},{288,16},{304,32},{320,48},{336,64},{352,80},{368,96},{384... | collective-permute-start | bytes 823304 | tf_op jit(solution)/shard_map/ppermute | solution.py:265
  14.0 2.9 %collective-permute-start.1 = (bf16[1072,128]{1,0:T(8,128)(2,1)}, bf16[1072,128]{1,0:T(8,128)(2,1)S(1)}, u32[]{:S(2)}, u32[]{:S(2)}) collective-permute-start(bf16[1072,128]{1,0:T(8,128)(2,1)} %pack.1.refs_0_), channel_id=1, source_target_pairs={{16,0},{32,16},{48,32},{64,48},{80,64},{96,80},{112,96},{128,112},... | collective-permute-start | bytes 823304 | tf_op jit(solution)/shard_map/ppermute | solution.py:265
  17.0 3.1 %collective-permute-start = (bf16[1072,128]{1,0:T(8,128)(2,1)}, bf16[1072,128]{1,0:T(8,128)(2,1)S(1)}, u32[]{:S(2)}, u32[]{:S(2)}) collective-permute-start(bf16[1072,128]{1,0:T(8,128)(2,1)} %pack.1.refs_0_), channel_id=1, source_target_pairs={{256,0},{272,16},{288,32},{304,48},{320,64},{336,80},{352,96},{368... | collective-permute-start | bytes 823304 | tf_op jit(solution)/shard_map/ppermute | solution.py:265
  20.1 0.9 multiply_convert_fusion.1
  20.9 30.2 %all_gather.6 = f16[128,2048]{1,0:T(8,128)(2,1)S(1)} all-gather(f16[16,2048]{1,0:T(8,128)(2,1)S(1)} %multiply_convert_fusion.1), channel_id=1, replica_groups={{0,32,64,96,128,160,192,224},{16,48,80,112,144,176,208,240},{256,288,32..., dimensions={0}, use_global_device_ids=true | all-gather | bytes 589824 | tf_op jit(solution)/shard_map/all_gather | solution.py:276
  51.2 0.1 multiply_convert_fusion.q_ref
  51.9 0.1 pad_add_fusion.place_ref
  52.0 0.0 collective-permute-done.2.refs_3_
  52.0 0.0 collective-permute-done.1.refs_2_
  52.0 0.0 collective-permute-done.refs_1_
  52.0 1.1 copy-done.1
  53.1 5.5 %attend.1 = bf16[128,2176]{1,0:T(8,128)(2,1)} custom-call(s32[2]{0:T(128)S(1)} %pad_add_fusion.place_ref, bf16[128,2048]{1,0:T(8,128)(2,1)S(1)} %multiply_convert_fusion.q_ref, bf16[1072,128]{1,0:T(8,128)(2,1)S(1)} %copy-done.1, bf16[1072,128]{1,0:T(8,128)(2,1)S(1)} %collective-permute-done.refs_1_, bf16[1072,128]{1,0:T(8,128)(2,1)S(1)} %collective-permute-done.1.refs_2_, ...), custom_call_target="tpu_custom_call" | custom-call | flops 3422552064 | bytes 4194304 | tf_op jit(solution)/shard_map/attend/pallas_call | solution.py:183
  58.6 8.1 %all-to-all-start = ((bf16[8,16,2176]{2,1,0:T(8,128)(2,1)}), bf16[8,16,2176]{2,1,0:T(8,128)(2,1)S(1)}, u32[]{:S(2)}, u32[]{:S(2)}) async-start(bf16[8,16,2176]{2,1,0:T(8,128)(2,1)} %bitcast.2), calls=%async_computation | async-start | bytes 1114112 | tf_op jit(solution)/shard_map/all_to_all | solution.py:283
  66.7 3.2 %collective-permute-start.3 = (bf16[2048,512]{1,0:T(8,128)(2,1)S(1)}, bf16[2048,512]{1,0:T(8,128)(2,1)}, u32[]{:S(2)}, u32[]{:S(2)}) collective-permute-start(bf16[2048,512]{1,0:T(8,128)(2,1)S(1)} %copy-done), channel_id=1, source_target_pairs={{0,256},{16,272},{32,288},{48,304},{64,320},{80,336},{96,352},{112... | collective-permute-start | bytes 6291464 | tf_op jit(solution)/shard_map/ppermute | solution.py:322
  69.9 21.5 %all-to-all-done = bf16[8,16,2176]{2,1,0:T(8,128)(2,1)S(1)} async-done(((bf16[8,16,2176]{2,1,0:T(8,128)(2,1)}), bf16[8,16,2176]{2,1,0:T(8,128)(2,1)S(1)}, u32[]{:S(2)}, u32[]{:S(2)}) %all-to-all-start) | async-done | bytes 557088 | tf_op jit(solution)/shard_map/all_to_all | solution.py:283
  91.3 0.5 merge.1
  91.8 34.0 %all-gather.1 = f16[256,2048]{1,0:T(8,128)(2,1)S(1)} all-gather(f16[16,2048]{1,0:T(8,128)(2,1)S(1)} %convert_element_type.27), channel_id=1, replica_groups={{0,16,32,48,64,80,96,112,128,144,160,176,192,208,224,240},{256,272,288,..., dimensions={0}, use_global_device_ids=true | all-gather | bytes 1114112 | tf_op jit(solution)/shard_map/all_gather | solution.py:323
  125.8 0.2 convert_element_type.28.rows_ref
  126.1 2.8 %project.1 = bf16[512,512]{1,0:T(8,128)(2,1)S(1)} custom-call(s32[1]{0:T(128)} %bitcast.place_ref, f32[16,128]{1,0:T(8,128)S(1)} %get-tuple-element.8.power_ref, bf16[256,2048]{1,0:T(8,128)(2,1)S(1)} %convert_element_type.28.rows_ref, bf16[2048,512]{1,0:T(8,128)(2,1)S(1)} %copy-done, bf16[2048,512]{1,0:T(8,128)(2,1)} %collective-permute-done.3.their_ref), custom_call_target="tpu_custom_call" | custom-call | flops 1073741824 | bytes 6291456 | tf_op jit(solution)/shard_map/project/pallas_call | solution.py:305
  128.9 11.7 %all_to_all.29 = bf16[4,128,512]{2,1,0:T(8,128)(2,1)S(1)} all-to-all(bf16[4,128,512]{2,1,0:T(8,128)(2,1)S(1)} %bitcast.9), channel_id=1, replica_groups={{0,2,256,258},{4,6,260,262},{8,10,264,266},{12,14,268,270},{16,18,272,2..., dimensions={0} | all-to-all | bytes 1048576 | tf_op jit(solution)/shard_map/all_to_all | solution.py:330
  140.6 0.1 bitcast_reduce_fusion
  140.7 11.0 %all_to_all.30 = bf16[4,64,512]{2,1,0:T(8,128)(2,1)S(1)} all-to-all(bf16[4,64,512]{2,1,0:T(8,128)(2,1)S(1)} %bitcast.10), channel_id=1, replica_groups={{0,4,8,12},{2,6,10,14},{1,5,9,13},{3,7,11,15},{16,20,24,28},{18,22,26,3..., dimensions={0} | all-to-all | bytes 524288 | tf_op jit(solution)/shard_map/all_to_all | solution.py:336
  151.7 0.7 convert_reduce_fusion
  (5 shorter events, 0.0 us)
Async XLA Ops:
  2.4 49.6 %collective-permute-start.2 = (bf16[1072,128]{1,0:T(8,128)(2,1)}, bf16[1072,128]{1,0:T(8,128)(2,1)S(1)}, u32[]{:S(2)}, u32[]{:S(2)}) collective-permute-start(bf16[1072,128]{1,0:T(8,128)(2,1)} %pack.1.refs_0_), channel_id=1, source_target_pairs={{272,0},{288,16},{304,32},{320,48},{336,64},{352,80},{368,96},{384... | collective-permute-start | bytes 823304 | tf_op jit(solution)/shard_map/ppermute | solution.py:265
  14.0 37.9 %collective-permute-start.1 = (bf16[1072,128]{1,0:T(8,128)(2,1)}, bf16[1072,128]{1,0:T(8,128)(2,1)S(1)}, u32[]{:S(2)}, u32[]{:S(2)}) collective-permute-start(bf16[1072,128]{1,0:T(8,128)(2,1)} %pack.1.refs_0_), channel_id=1, source_target_pairs={{16,0},{32,16},{48,32},{64,48},{80,64},{96,80},{112,96},{128,112},... | collective-permute-start | bytes 823304 | tf_op jit(solution)/shard_map/ppermute | solution.py:265
  17.0 35.0 %collective-permute-start = (bf16[1072,128]{1,0:T(8,128)(2,1)}, bf16[1072,128]{1,0:T(8,128)(2,1)S(1)}, u32[]{:S(2)}, u32[]{:S(2)}) collective-permute-start(bf16[1072,128]{1,0:T(8,128)(2,1)} %pack.1.refs_0_), channel_id=1, source_target_pairs={{256,0},{272,16},{288,32},{304,48},{320,64},{336,80},{352,96},{368... | collective-permute-start | bytes 823304 | tf_op jit(solution)/shard_map/ppermute | solution.py:265
  52.0 14.7 %copy-start = (bf16[2048,512]{1,0:T(8,128)(2,1)S(1)}, bf16[2048,512]{1,0:T(8,128)(2,1)}, u32[]{:S(2)}) copy-start(bf16[2048,512]{1,0:T(8,128)(2,1)} %weight_ref.1) | copy-start | bytes 6291460
  52.0 1.1 copy-start.1
  58.6 32.8 %all-to-all-start = ((bf16[8,16,2176]{2,1,0:T(8,128)(2,1)}), bf16[8,16,2176]{2,1,0:T(8,128)(2,1)S(1)}, u32[]{:S(2)}, u32[]{:S(2)}) async-start(bf16[8,16,2176]{2,1,0:T(8,128)(2,1)} %bitcast.2), calls=%async_computation | async-start | bytes 1114112 | tf_op jit(solution)/shard_map/all_to_all | solution.py:283
  66.7 59.4 %collective-permute-start.3 = (bf16[2048,512]{1,0:T(8,128)(2,1)S(1)}, bf16[2048,512]{1,0:T(8,128)(2,1)}, u32[]{:S(2)}, u32[]{:S(2)}) collective-permute-start(bf16[2048,512]{1,0:T(8,128)(2,1)S(1)} %copy-done), channel_id=1, source_target_pairs={{0,256},{16,272},{32,288},{48,304},{64,320},{80,336},{96,352},{112... | collective-permute-start | bytes 6291464 | tf_op jit(solution)/shard_map/ppermute | solution.py:322
